TPU v7x, 32 devices: a whole 2x2x4 slice. The times are simulated.
32 devices in a mesh: gx: 4 (over y, x), gy: 4 (over z), gz: 2 (over core).
Axes of the slice: x: 2, y: 2, z: 4, core: 2. Of those that a mesh axis runs over, the one named last changes fastest.
Arguments:
- phase: int32 [32, 256, 256], P('gx', 'gy', 'gz'), may hold values 0 or 1
- density: float32 [32, 256, 256], P('gx', 'gy', 'gz'), may hold values from 0.5 to 2
- rhs: float32 [1, 32, 256, 256], P(None, 'gx', 'gy', 'gz'), may hold values from -6 to 6
Outputs:
- scaled_solution: float32 [1, 32, 256, 256], P(None, 'gx', 'gy', 'gz')
- residual: float32 [1, 32, 256, 256], P(None, 'gx', 'gy', 'gz')
All inputs are finite; a program needn't handle non-finite values. No bound on the sum of `phase` on one device may be relied on, other than what follows from the above.
Results may differ from a plain program's by a relative error of at most 0.0003.
Values sent between devices are 32-bit elements; how exact they have to be, the bound alone decides.
No kernel may reach another device: no remote copies, remote signals or barrier semaphores. Data moves between devices by JAX's collectives and lax.ppermute only.
A program may use at most 128 MiB of HBM per device.

v0:
```python
import jax
import jax.numpy as jnp
from jax import lax
from jax.sharding import PartitionSpec as P

LEVELS = 4
SWEEPS = 2
COARSE_SWEEPS = 4


damping = 2.0 / 3.0


def padded_2(cells, sides, width):
    for axis, dim in sides:
        count = lax.axis_size(axis)
        ends = count - 1
        head = lax.slice_in_dim(cells, 0, width, axis=dim)
        tail = lax.slice_in_dim(cells, cells.shape[dim] - width, cells.shape[dim], axis=dim)
        cells = jnp.concatenate(
            [
                lax.ppermute(tail, axis, [(i, (i + 1) % count) for i in range(ends)]),
                cells,
                lax.ppermute(head, axis, [((i + 1) % count, i) for i in range(ends)]),
            ],
            axis=dim,
        )
    return cells


def face_pair(rho, up_nb, down_nb, top, bottom):
    face_up = 2.0 / (rho + up_nb)
    face_down = 2.0 / (rho + down_nb)
    return (face_up, face_down, jnp.where(top, 0.0, face_up), jnp.where(bottom, 0.0, face_down))


def side_masks(where_now, axis_count, count, shape, dim):
    row = lax.broadcasted_iota(jnp.int32, shape, dim)
    top = (row == count - 1) & (where_now == axis_count - 1)
    bottom = (row == 0) & (where_now == 0)
    return (top, bottom)


def make_coef(rho):
    nx, ny, nz = rho.shape
    ext = padded_2(rho, (("gx", 0), ("gy", 1), ("gz", 2)), 1)
    top_x, bot_x = side_masks(lax.axis_index("gx"), lax.axis_size("gx"), nx, (nx, 1, 1), 0)
    top_y, bot_y = side_masks(lax.axis_index("gy"), lax.axis_size("gy"), ny, (1, ny, 1), 1)
    top_z, bot_z = side_masks(lax.axis_index("gz"), lax.axis_size("gz"), nz, (1, 1, nz), 2)
    fxu, fxd, kxu, kxd = face_pair(
        rho,
        jnp.where(top_x, rho, ext[2:, 1:-1, 1:-1]),
        jnp.where(bot_x, rho, ext[:-2, 1:-1, 1:-1]),
        top_x,
        bot_x,
    )
    fyu, fyd, kyu, kyd = face_pair(
        rho,
        jnp.where(top_y, rho, ext[1:-1, 2:, 1:-1]),
        jnp.where(bot_y, rho, ext[1:-1, :-2, 1:-1]),
        top_y,
        bot_y,
    )
    fzu, fzd, kzu, kzd = face_pair(
        rho,
        jnp.where(top_z, rho, ext[1:-1, 1:-1, 2:]),
        jnp.where(bot_z, rho, ext[1:-1, 1:-1, :-2]),
        top_z,
        bot_z,
    )
    diag = fxu + fxd + fyu + fyd + fzu + fzd
    return jnp.stack([diag, kxu, kxd, kyu, kyd, kzu, kzd])


def blocks(a):
    s = a.shape
    lead = s[:-3]
    return a.reshape(lead + (s[-3] // 2, 2, s[-2] // 2, 2, s[-1] // 2, 2)).sum(axis=(-5, -3, -1))


def prolong(e):
    s = e.shape
    lead = s[:-3]
    wide = e.reshape(lead + (s[-3], 1, s[-2], 1, s[-1], 1))
    wide = jnp.broadcast_to(wide, lead + (s[-3], 2, s[-2], 2, s[-1], 2))
    return wide.reshape(lead + (2 * s[-3], 2 * s[-2], 2 * s[-1]))


def face_x(a, offset):
    b = a[offset::2]
    n0, n1, n2 = b.shape
    return b.reshape(n0, n1 // 2, 2, n2 // 2, 2).sum(axis=(2, 4))


def face_y(a, offset):
    b = a[:, offset::2]
    n0, n1, n2 = b.shape
    return b.reshape(n0 // 2, 2, n1, n2 // 2, 2).sum(axis=(1, 4))


def face_z(a, offset):
    b = a[:, :, offset::2]
    n0, n1, n2 = b.shape
    return b.reshape(n0 // 2, 2, n1 // 2, 2, n2).sum(axis=(1, 3))


def coarsen(coef):
    inner = face_x(coef[1], 0) + face_y(coef[3], 0) + face_z(coef[5], 0)
    diag = blocks(coef[0]) - 2.0 * inner
    return jnp.stack(
        [
            diag,
            face_x(coef[1], 1),
            face_x(coef[2], 0),
            face_y(coef[3], 1),
            face_y(coef[4], 0),
            face_z(coef[5], 1),
            face_z(coef[6], 0),
        ]
    )


def stencil(padded, field, coef):
    beside = coef[1] * padded[:, 2:, 1:-1, 1:-1] + coef[2] * padded[:, :-2, 1:-1, 1:-1]
    beside = beside + coef[3] * padded[:, 1:-1, 2:, 1:-1] + coef[4] * padded[:, 1:-1, :-2, 1:-1]
    beside = beside + coef[5] * padded[:, 1:-1, 1:-1, 2:] + coef[6] * padded[:, 1:-1, 1:-1, :-2]
    return coef[0] * field - beside


def pad_spread(field):
    return padded_2(field, (("gx", 1), ("gy", 2), ("gz", 3)), 1)


def sweep(field, source, coef, pad_fn, first):
    if first:
        change = source
    else:
        change = source - stencil(pad_fn(field), field, coef)
    return field + damping * change / coef[0]


def smooth_many(source, coef, pad_fn, count):
    field = jnp.zeros_like(source)
    for step in range(count):
        field = sweep(field, source, coef, pad_fn, step == 0)
    return field


def coarsest(source, coef):
    return smooth_many(source, coef, pad_spread, COARSE_SWEEPS)


def vcycle(level, source, coefs):
    coef = coefs[level]
    if level == LEVELS - 1:
        return coarsest(source, coef)
    field = smooth_many(source, coef, pad_spread, SWEEPS)
    remain = source - stencil(pad_spread(field), field, coef)
    correction = vcycle(level + 1, blocks(remain), coefs)
    field = field + prolong(correction)
    for step in range(SWEEPS):
        field = sweep(field, source, coef, pad_spread, False)
    return field


def on_device(phase, density, rhs):
    rho = jnp.where(phase == 1, 1000.0, 1.0).astype(jnp.float32) * density
    coefs = [make_coef(rho)]
    for level in range(LEVELS - 1):
        coefs.append(coarsen(coefs[-1]))
    solution = vcycle(0, rhs, coefs)
    scaled_solution = coefs[0][0] * solution
    residual = rhs - stencil(pad_spread(solution), solution, coefs[0])
    return (scaled_solution, residual)


def solution(mesh):
    in_specs = (P("gx", "gy", "gz"), P("gx", "gy", "gz"), P(None, "gx", "gy", "gz"))
    out_specs = (P(None, "gx", "gy", "gz"), P(None, "gx", "gy", "gz"))
    return jax.shard_map(
        on_device, mesh=mesh, in_specs=in_specs, out_specs=out_specs, check_vma=False
    )
```

profile of v0, /device:TPU:29, one launch (start us, length us, event | category | flops | bytes accessed | tf_op | source)
XLA Modules:
  0.0 556.4 jit_solution(10489099055664752276)
XLA Ops:
  11.7 4.0 collective-permute-start.2
  16.7 5.2 collective-permute-start.4
  28.8 3.4 collective-permute-start.7
  34.4 3.9 collective-permute-start.8
  44.2 4.7 collective-permute-start.10
  52.7 3.4 collective-permute-start.13
  61.7 18.1 %reshape_squeeze_stack.2 = f32[4,2,32,2,64,2]{5,4,3,2,1,0:T(8,128)} reshape(f32[8,64,128]{2,1,0:T(8,128)S(1)} %get-tuple-element.18) | data formatting | bytes 524288 | tf_op jit(solution)/shard_map/reshape;squeeze;stack | solution.py:78
  79.7 7.6 %reduce_sum.361 = f32[4,32,64]{2,1,0:T(8,128)} reduce(f32[4,2,32,2,64,2]{5,4,3,2,1,0:T(8,128)} %reshape_squeeze_stack.2, f32[]{:T(128)} %constant.5.clone.1), dimensions={1,3,5}, to_apply=%region_1.2 | reduce | flops 57344 | bytes 294916 | tf_op jit(solution)/shard_map/reduce_sum | solution.py:78
  89.7 5.3 collective-permute-start.16
  95.7 4.5 slice.794
  103.7 5.6 %reduce_sum.362 = f32[4,32,64]{0,2,1:T(8,128)S(1)} reduce(f32[4,32,2,64,2]{0,4,3,2,1:T(2,128)} %bitcast.352, f32[]{:T(128)} %constant.5.clone.1), dimensions={2,4}, to_apply=%region_2.3 | reduce | flops 24576 | bytes 163844 | tf_op jit(solution)/shard_map/reduce_sum | solution.py:92
  112.5 18.1 %reshape.474 = f32[4,2,32,2,64,2]{5,4,3,2,1,0:T(8,128)} reshape(f32[1,8,64,128]{3,2,1,0:T(8,128)S(1)} %fusion.54) | data formatting | bytes 524288 | tf_op jit(solution)/shard_map/reshape | solution.py:78
  130.6 7.0 %reduce_sum.359 = f32[4,32,64]{2,1,0:T(8,128)S(1)} reduce(f32[4,2,32,2,64,2]{5,4,3,2,1,0:T(8,128)} %reshape.474, f32[]{:T(128)} %constant.5.clone.1), dimensions={1,3,5}, to_apply=%region_0.1 | reduce | flops 57344 | bytes 294916 | tf_op jit(solution)/shard_map/reduce_sum | solution.py:78
  140.2 3.4 collective-permute-start.19
  147.0 5.3 collective-permute-start.20
  152.3 4.5 slice.810
  156.8 4.5 slice.807
  174.5 5.6 %reduce_sum.366 = f32[4,32,64]{0,2,1:T(8,128)S(1)} reduce(f32[4,32,2,64,2]{0,4,3,2,1:T(2,128)} %bitcast.353, f32[]{:T(128)} %constant.5.clone.1), dimensions={2,4}, to_apply=%region_6.7 | reduce | flops 24576 | bytes 163844 | tf_op jit(solution)/shard_map/reduce_sum | solution.py:92
  181.2 3.5 copy.288
  184.7 5.6 %reduce_sum.365 = f32[4,32,64]{0,2,1:T(8,128)S(1)} reduce(f32[4,32,2,64,2]{0,4,3,2,1:T(2,128)} %bitcast.354, f32[]{:T(128)} %constant.5.clone.1), dimensions={2,4}, to_apply=%region_5.6 | reduce | flops 24576 | bytes 163844 | tf_op jit(solution)/shard_map/reduce_sum | solution.py:92
  195.9 3.4 collective-permute-start.25
  203.9 5.0 collective-permute-start.26
  224.4 4.3 sub.180
  231.9 5.1 collective-permute-start.28
  243.6 4.3 reshape.484
  253.6 3.9 collective-permute-start.31
  265.1 5.5 slice.831
  270.6 3.4 slice.828
  287.4 3.9 collective-permute-start.34
  302.0 4.3 collective-permute-start.38
  312.0 4.4 collective-permute-start.40
  332.9 4.8 collective-permute-start.46
  353.1 4.8 collective-permute-start.52
  373.4 4.8 collective-permute-start.58
  394.0 4.8 collective-permute-start.64
  414.4 4.8 collective-permute-start.70
  433.7 4.0 collective-permute-start.74
  438.8 4.5 collective-permute-start.76
  454.6 3.9 collective-permute-start.80
  463.2 4.7 collective-permute-start.82
  471.6 6.5 %broadcast_in_dim.131 = f32[4,2,32,2,64,2]{5,4,3,2,1,0:T(8,128)} broadcast(f32[4,32,64]{2,1,0:T(8,128)S(1)} %fusion.133), dimensions={0,2,4} | broadcast | bytes 294912 | tf_op jit(solution)/shard_map/broadcast_in_dim | solution.py:85
  478.1 12.6 %broadcast_in_dim.132 = f32[1,8,64,128]{3,2,1,0:T(8,128)S(1)} reshape(f32[4,2,32,2,64,2]{5,4,3,2,1,0:T(8,128)} %broadcast_in_dim.131) | data formatting | bytes 524288 | tf_op jit(solution)/shard_map/broadcast_in_dim | solution.py:85
  492.7 3.4 collective-permute-start.85
  505.8 4.7 collective-permute-start.88
  514.2 3.4 collective-permute-start.91
  527.3 4.9 collective-permute-start.94
  535.8 3.4 collective-permute-start.97
  548.9 4.9 collective-permute-start.100
  (409 shorter events, 297.9 us)
Async XLA Ops:
  4.8 5.6 collective-permute-start.1
  16.7 6.5 %collective-permute-start.4 = (f32[10,66,1]{2,1,0:T(8,128)S(1)}, f32[10,66,1]{2,1,0:T(8,128)S(1)}, u32[]{:S(2)}, u32[]{:S(2)}) collective-permute-start(f32[10,66,1]{2,1,0:T(8,128)S(1)} %get-tuple-element.32), channel_id=1, source_target_pairs={{1,0},{3,2},{5,4},{7,6},{9,8},{11,10},{13,12},{15,14},{17,16},{19,... | collective-permute-start | bytes 7928 | tf_op jit(solution)/shard_map/ppermute | solution.py:24
  28.8 5.6 collective-permute-start.7
  42.9 6.0 %collective-permute-start.11 = (f32[1,10,66,1]{3,2,1,0:T(8,128)S(1)}, f32[1,10,66,1]{3,2,1,0:T(8,128)S(1)}, u32[]{:S(2)}, u32[]{:S(2)}) collective-permute-start(f32[1,10,66,1]{3,2,1,0:T(8,128)S(1)} %get-tuple-element.30), channel_id=1, source_target_pairs={{0,1},{2,3},{4,5},{6,7},{8,9},{10,11},{12,13},{14,15},{16,17},{18,... | collective-permute-start | bytes 7928 | tf_op jit(solution)/shard_map/ppermute | solution.py:22
  44.2 6.0 %collective-permute-start.10 = (f32[1,10,66,1]{3,2,1,0:T(8,128)S(1)}, f32[1,10,66,1]{3,2,1,0:T(8,128)S(1)}, u32[]{:S(2)}, u32[]{:S(2)}) collective-permute-start(f32[1,10,66,1]{3,2,1,0:T(8,128)S(1)} %get-tuple-element.29), channel_id=1, source_target_pairs={{1,0},{3,2},{5,4},{7,6},{9,8},{11,10},{13,12},{15,14},{17,16},{19,... | collective-permute-start | bytes 7928 | tf_op jit(solution)/shard_map/ppermute | solution.py:24
  52.7 5.6 collective-permute-start.13
  58.3 29.1 %collective-permute-start.14 = (f32[1,10,1,128]{3,2,1,0:T(1,128)S(1)}, f32[1,10,1,128]{3,2,1,0:T(1,128)S(1)}, u32[]{:S(2)}, u32[]{:S(2)}) collective-permute-start(f32[1,10,1,128]{3,2,1,0:T(1,128)S(1)} %get-tuple-element.40), channel_id=1, source_target_pairs={{2,0},{4,2},{6,4},{3,1},{5,3},{7,5},{10,8},{12,10},{14,12},{11,9},... | collective-permute-start | bytes 15368 | tf_op jit(solution)/shard_map/ppermute | solution.py:24
  60.4 27.0 %collective-permute-start.15 = (f32[1,10,1,128]{3,2,1,0:T(1,128)S(1)}, f32[1,10,1,128]{3,2,1,0:T(1,128)S(1)}, u32[]{:S(2)}, u32[]{:S(2)}) collective-permute-start(f32[1,10,1,128]{3,2,1,0:T(1,128)S(1)} %get-tuple-element.39), channel_id=1, source_target_pairs={{0,2},{2,4},{4,6},{1,3},{3,5},{5,7},{8,10},{10,12},{12,14},{9,11},... | collective-permute-start | bytes 15368 | tf_op jit(solution)/shard_map/ppermute | solution.py:22
  88.4 22.7 %collective-permute-start.17 = (f32[1,10,66,1]{3,2,1,0:T(8,128)}, f32[1,10,66,1]{3,2,1,0:T(8,128)}, u32[]{:S(2)}, u32[]{:S(2)}) collective-permute-start(f32[1,10,66,1]{3,2,1,0:T(8,128)} %get-tuple-element.28), channel_id=1, source_target_pairs={{0,1},{2,3},{4,5},{6,7},{8,9},{10,11},{12,13},{14,15},{16,17},{18,... | collective-permute-start | bytes 7928 | tf_op jit(solution)/shard_map/ppermute | solution.py:22
  89.7 21.5 %collective-permute-start.16 = (f32[1,10,66,1]{3,2,1,0:T(8,128)}, f32[1,10,66,1]{3,2,1,0:T(8,128)}, u32[]{:S(2)}, u32[]{:S(2)}) collective-permute-start(f32[1,10,66,1]{3,2,1,0:T(8,128)} %get-tuple-element.27), channel_id=1, source_target_pairs={{1,0},{3,2},{5,4},{7,6},{9,8},{11,10},{13,12},{15,14},{17,16},{19,... | collective-permute-start | bytes 7928 | tf_op jit(solution)/shard_map/ppermute | solution.py:24
  145.7 18.6 %collective-permute-start.21 = (f32[1,6,1,64]{3,2,1,0:T(1,128)S(1)}, f32[1,6,1,64]{3,2,1,0:T(1,128)S(1)}, u32[]{:S(2)}, u32[]{:S(2)}) collective-permute-start(f32[1,6,1,64]{3,2,1,0:T(1,128)S(1)} %get-tuple-element.82), channel_id=1, source_target_pairs={{0,2},{2,4},{4,6},{1,3},{3,5},{5,7},{8,10},{10,12},{12,14},{9,11},... | collective-permute-start | bytes 4616 | tf_op jit(solution)/shard_map/ppermute | solution.py:22
  147.0 17.4 %collective-permute-start.20 = (f32[1,6,1,64]{3,2,1,0:T(1,128)S(1)}, f32[1,6,1,64]{3,2,1,0:T(1,128)S(1)}, u32[]{:S(2)}, u32[]{:S(2)}) collective-permute-start(f32[1,6,1,64]{3,2,1,0:T(1,128)S(1)} %get-tuple-element.81), channel_id=1, source_target_pairs={{2,0},{4,2},{6,4},{3,1},{5,3},{7,5},{10,8},{12,10},{14,12},{11,9},... | collective-permute-start | bytes 4616 | tf_op jit(solution)/shard_map/ppermute | solution.py:24
  165.4 25.9 %collective-permute-start.22 = (f32[1,6,34,1]{3,0,2,1:T(1,128)}, f32[1,6,34,1]{3,0,2,1:T(1,128)}, u32[]{:S(2)}, u32[]{:S(2)}) collective-permute-start(f32[1,6,34,1]{3,0,2,1:T(1,128)} %get-tuple-element.73), channel_id=1, source_target_pairs={{1,0},{3,2},{5,4},{7,6},{9,8},{11,10},{13,12},{15,14},{17,16},{19,... | collective-permute-start | bytes 2456 | tf_op jit(solution)/shard_map/ppermute | solution.py:24
  168.0 23.3 %collective-permute-start.23 = (f32[1,6,34,1]{3,0,2,1:T(1,128)}, f32[1,6,34,1]{3,0,2,1:T(1,128)}, u32[]{:S(2)}, u32[]{:S(2)}) collective-permute-start(f32[1,6,34,1]{3,0,2,1:T(1,128)} %get-tuple-element.74), channel_id=1, source_target_pairs={{0,1},{2,3},{4,5},{6,7},{8,9},{10,11},{12,13},{14,15},{16,17},{18,... | collective-permute-start | bytes 2456 | tf_op jit(solution)/shard_map/ppermute | solution.py:22
  202.6 28.0 %collective-permute-start.27 = (f32[1,6,1,64]{3,2,1,0:T(1,128)}, f32[1,6,1,64]{3,2,1,0:T(1,128)}, u32[]{:S(2)}, u32[]{:S(2)}) collective-permute-start(f32[1,6,1,64]{3,2,1,0:T(1,128)} %get-tuple-element.80), channel_id=1, source_target_pairs={{0,2},{2,4},{4,6},{1,3},{3,5},{5,7},{8,10},{10,12},{12,14},{9,11},... | collective-permute-start | bytes 4616 | tf_op jit(solution)/shard_map/ppermute | solution.py:22
  203.9 26.7 %collective-permute-start.26 = (f32[1,6,1,64]{3,2,1,0:T(1,128)}, f32[1,6,1,64]{3,2,1,0:T(1,128)}, u32[]{:S(2)}, u32[]{:S(2)}) collective-permute-start(f32[1,6,1,64]{3,2,1,0:T(1,128)} %get-tuple-element.79), channel_id=1, source_target_pairs={{2,0},{4,2},{6,4},{3,1},{5,3},{7,5},{10,8},{12,10},{14,12},{11,9},... | collective-permute-start | bytes 4616 | tf_op jit(solution)/shard_map/ppermute | solution.py:24
  231.9 8.4 %collective-permute-start.28 = (f32[1,6,34,1]{3,0,2,1:T(1,128)S(1)}, f32[1,6,34,1]{3,0,2,1:T(1,128)S(1)}, u32[]{:S(2)}, u32[]{:S(2)}) collective-permute-start(f32[1,6,34,1]{3,0,2,1:T(1,128)S(1)} %get-tuple-element.69), channel_id=1, source_target_pairs={{1,0},{3,2},{5,4},{7,6},{9,8},{11,10},{13,12},{15,14},{17,16},{19,... | collective-permute-start | bytes 2456 | tf_op jit(solution)/shard_map/ppermute | solution.py:24
  251.7 23.2 %collective-permute-start.30 = (f32[1,1,16,32]{3,2,1,0:T(8,128)}, f32[1,1,16,32]{3,2,1,0:T(8,128)}, u32[]{:S(2)}, u32[]{:S(2)}) collective-permute-start(f32[1,1,16,32]{3,2,1,0:T(8,128)} %get-tuple-element.122), channel_id=1, source_target_pairs={{8,0},{16,8},{24,16},{9,1},{17,9},{25,17},{10,2},{18,10},{26,18},{... | collective-permute-start | bytes 6152 | tf_op jit(solution)/shard_map/ppermute | solution.py:24
  253.6 21.3 %collective-permute-start.31 = (f32[1,1,16,32]{3,2,1,0:T(8,128)}, f32[1,1,16,32]{3,2,1,0:T(8,128)}, u32[]{:S(2)}, u32[]{:S(2)}) collective-permute-start(f32[1,1,16,32]{3,2,1,0:T(8,128)} %get-tuple-element.121), channel_id=1, source_target_pairs={{0,8},{8,16},{16,24},{1,9},{9,17},{17,25},{2,10},{10,18},{18,26},{... | collective-permute-start | bytes 6152 | tf_op jit(solution)/shard_map/ppermute | solution.py:22
  275.6 9.6 %collective-permute-start.32 = (f32[1,4,1,32]{3,2,1,0:T(1,128)S(1)}, f32[1,4,1,32]{3,2,1,0:T(1,128)S(1)}, u32[]{:S(2)}, u32[]{:S(2)}) collective-permute-start(f32[1,4,1,32]{3,2,1,0:T(1,128)S(1)} %get-tuple-element.106), channel_id=1, source_target_pairs={{2,0},{4,2},{6,4},{3,1},{5,3},{7,5},{10,8},{12,10},{14,12},{11,9},... | collective-permute-start | bytes 1544 | tf_op jit(solution)/shard_map/ppermute | solution.py:24
  278.8 6.5 %collective-permute-start.33 = (f32[1,4,1,32]{3,2,1,0:T(1,128)S(1)}, f32[1,4,1,32]{3,2,1,0:T(1,128)S(1)}, u32[]{:S(2)}, u32[]{:S(2)}) collective-permute-start(f32[1,4,1,32]{3,2,1,0:T(1,128)S(1)} %get-tuple-element.105), channel_id=1, source_target_pairs={{0,2},{2,4},{4,6},{1,3},{3,5},{5,7},{8,10},{10,12},{12,14},{9,11},... | collective-permute-start | bytes 1544 | tf_op jit(solution)/shard_map/ppermute | solution.py:22
  286.1 7.6 %collective-permute-start.35 = (f32[1,4,18,1]{3,2,1,0:T(8,128)S(1)}, f32[1,4,18,1]{3,2,1,0:T(8,128)S(1)}, u32[]{:S(2)}, u32[]{:S(2)}) collective-permute-start(f32[1,4,18,1]{3,2,1,0:T(8,128)S(1)} %get-tuple-element.98), channel_id=1, source_target_pairs={{0,1},{2,3},{4,5},{6,7},{8,9},{10,11},{12,13},{14,15},{16,17},{18,... | collective-permute-start | bytes 872 | tf_op jit(solution)/shard_map/ppermute | solution.py:22
  287.4 6.3 %collective-permute-start.34 = (f32[1,4,18,1]{3,2,1,0:T(8,128)S(1)}, f32[1,4,18,1]{3,2,1,0:T(8,128)S(1)}, u32[]{:S(2)}, u32[]{:S(2)}) collective-permute-start(f32[1,4,18,1]{3,2,1,0:T(8,128)S(1)} %get-tuple-element.97), channel_id=1, source_target_pairs={{1,0},{3,2},{5,4},{7,6},{9,8},{11,10},{13,12},{15,14},{17,16},{19,... | collective-permute-start | bytes 872 | tf_op jit(solution)/shard_map/ppermute | solution.py:24
  294.7 6.4 %collective-permute-start.36 = (f32[1,1,16,32]{3,2,1,0:T(8,128)S(1)}, f32[1,1,16,32]{3,2,1,0:T(8,128)S(1)}, u32[]{:S(2)}, u32[]{:S(2)}) collective-permute-start(f32[1,1,16,32]{3,2,1,0:T(8,128)S(1)} %get-tuple-element.120), channel_id=1, source_target_pairs={{8,0},{16,8},{24,16},{9,1},{17,9},{25,17},{10,2},{18,10},{26,18},{... | collective-permute-start | bytes 6152 | tf_op jit(solution)/shard_map/ppermute | solution.py:24
  302.0 5.7 %collective-permute-start.38 = (f32[1,4,1,32]{3,2,1,0:T(1,128)S(1)}, f32[1,4,1,32]{3,2,1,0:T(1,128)S(1)}, u32[]{:S(2)}, u32[]{:S(2)}) collective-permute-start(f32[1,4,1,32]{3,2,1,0:T(1,128)S(1)} %get-tuple-element.104), channel_id=1, source_target_pairs={{2,0},{4,2},{6,4},{3,1},{5,3},{7,5},{10,8},{12,10},{14,12},{11,9},... | collective-permute-start | bytes 1544 | tf_op jit(solution)/shard_map/ppermute | solution.py:24
  310.7 5.9 %collective-permute-start.41 = (f32[1,4,18,1]{3,2,1,0:T(8,128)S(1)}, f32[1,4,18,1]{3,2,1,0:T(8,128)S(1)}, u32[]{:S(2)}, u32[]{:S(2)}) collective-permute-start(f32[1,4,18,1]{3,2,1,0:T(8,128)S(1)} %get-tuple-element.96), channel_id=1, source_target_pairs={{0,1},{2,3},{4,5},{6,7},{8,9},{10,11},{12,13},{14,15},{16,17},{18,... | collective-permute-start | bytes 872 | tf_op jit(solution)/shard_map/ppermute | solution.py:22
  317.3 5.7 %collective-permute-start.42 = (f32[1,1,8,16]{3,2,1,0:T(8,128)S(1)}, f32[1,1,8,16]{3,2,1,0:T(8,128)S(1)}, u32[]{:S(2)}, u32[]{:S(2)}) collective-permute-start(f32[1,1,8,16]{3,2,1,0:T(8,128)S(1)} %get-tuple-element.4), channel_id=1, source_target_pairs={{8,0},{16,8},{24,16},{9,1},{17,9},{25,17},{10,2},{18,10},{26,18},{... | collective-permute-start | bytes 1544 | tf_op jit(solution)/shard_map/ppermute | solution.py:24
  331.6 6.2 %collective-permute-start.47 = (f32[1,3,10,1]{3,2,1,0:T(8,128)S(1)}, f32[1,3,10,1]{3,2,1,0:T(8,128)S(1)}, u32[]{:S(2)}, u32[]{:S(2)}) collective-permute-start(f32[1,3,10,1]{3,2,1,0:T(8,128)S(1)} %get-tuple-element.112), channel_id=1, source_target_pairs={{0,1},{2,3},{4,5},{6,7},{8,9},{10,11},{12,13},{14,15},{16,17},{18,... | collective-permute-start | bytes 368 | tf_op jit(solution)/shard_map/ppermute | solution.py:22
  332.9 5.7 %collective-permute-start.46 = (f32[1,3,10,1]{3,2,1,0:T(8,128)S(1)}, f32[1,3,10,1]{3,2,1,0:T(8,128)S(1)}, u32[]{:S(2)}, u32[]{:S(2)}) collective-permute-start(f32[1,3,10,1]{3,2,1,0:T(8,128)S(1)} %get-tuple-element.111), channel_id=1, source_target_pairs={{1,0},{3,2},{5,4},{7,6},{9,8},{11,10},{13,12},{15,14},{17,16},{19,... | collective-permute-start | bytes 368 | tf_op jit(solution)/shard_map/ppermute | solution.py:24
  351.8 6.1 %collective-permute-start.53 = (f32[1,3,10,1]{3,2,1,0:T(8,128)S(1)}, f32[1,3,10,1]{3,2,1,0:T(8,128)S(1)}, u32[]{:S(2)}, u32[]{:S(2)}) collective-permute-start(f32[1,3,10,1]{3,2,1,0:T(8,128)S(1)} %get-tuple-element.110), channel_id=1, source_target_pairs={{0,1},{2,3},{4,5},{6,7},{8,9},{10,11},{12,13},{14,15},{16,17},{18,... | collective-permute-start | bytes 368 | tf_op jit(solution)/shard_map/ppermute | solution.py:22
  353.1 5.7 %collective-permute-start.52 = (f32[1,3,10,1]{3,2,1,0:T(8,128)S(1)}, f32[1,3,10,1]{3,2,1,0:T(8,128)S(1)}, u32[]{:S(2)}, u32[]{:S(2)}) collective-permute-start(f32[1,3,10,1]{3,2,1,0:T(8,128)S(1)} %get-tuple-element.109), channel_id=1, source_target_pairs={{1,0},{3,2},{5,4},{7,6},{9,8},{11,10},{13,12},{15,14},{17,16},{19,... | collective-permute-start | bytes 368 | tf_op jit(solution)/shard_map/ppermute | solution.py:24
  372.1 6.1 %collective-permute-start.59 = (f32[1,3,10,1]{3,2,1,0:T(8,128)S(1)}, f32[1,3,10,1]{3,2,1,0:T(8,128)S(1)}, u32[]{:S(2)}, u32[]{:S(2)}) collective-permute-start(f32[1,3,10,1]{3,2,1,0:T(8,128)S(1)} %get-tuple-element.108), channel_id=1, source_target_pairs={{0,1},{2,3},{4,5},{6,7},{8,9},{10,11},{12,13},{14,15},{16,17},{18,... | collective-permute-start | bytes 368 | tf_op jit(solution)/shard_map/ppermute | solution.py:22
  373.4 5.7 %collective-permute-start.58 = (f32[1,3,10,1]{3,2,1,0:T(8,128)S(1)}, f32[1,3,10,1]{3,2,1,0:T(8,128)S(1)}, u32[]{:S(2)}, u32[]{:S(2)}) collective-permute-start(f32[1,3,10,1]{3,2,1,0:T(8,128)S(1)} %get-tuple-element.107), channel_id=1, source_target_pairs={{1,0},{3,2},{5,4},{7,6},{9,8},{11,10},{13,12},{15,14},{17,16},{19,... | collective-permute-start | bytes 368 | tf_op jit(solution)/shard_map/ppermute | solution.py:24
  392.7 6.1 %collective-permute-start.65 = (f32[1,4,18,1]{3,2,1,0:T(8,128)S(1)}, f32[1,4,18,1]{3,2,1,0:T(8,128)S(1)}, u32[]{:S(2)}, u32[]{:S(2)}) collective-permute-start(f32[1,4,18,1]{3,2,1,0:T(8,128)S(1)} %get-tuple-element.94), channel_id=1, source_target_pairs={{0,1},{2,3},{4,5},{6,7},{8,9},{10,11},{12,13},{14,15},{16,17},{18,... | collective-permute-start | bytes 872 | tf_op jit(solution)/shard_map/ppermute | solution.py:22
  394.0 5.7 %collective-permute-start.64 = (f32[1,4,18,1]{3,2,1,0:T(8,128)S(1)}, f32[1,4,18,1]{3,2,1,0:T(8,128)S(1)}, u32[]{:S(2)}, u32[]{:S(2)}) collective-permute-start(f32[1,4,18,1]{3,2,1,0:T(8,128)S(1)} %get-tuple-element.93), channel_id=1, source_target_pairs={{1,0},{3,2},{5,4},{7,6},{9,8},{11,10},{13,12},{15,14},{17,16},{19,... | collective-permute-start | bytes 872 | tf_op jit(solution)/shard_map/ppermute | solution.py:24
  413.1 6.1 %collective-permute-start.71 = (f32[1,4,18,1]{3,2,1,0:T(8,128)S(1)}, f32[1,4,18,1]{3,2,1,0:T(8,128)S(1)}, u32[]{:S(2)}, u32[]{:S(2)}) collective-permute-start(f32[1,4,18,1]{3,2,1,0:T(8,128)S(1)} %get-tuple-element.92), channel_id=1, source_target_pairs={{0,1},{2,3},{4,5},{6,7},{8,9},{10,11},{12,13},{14,15},{16,17},{18,... | collective-permute-start | bytes 872 | tf_op jit(solution)/shard_map/ppermute | solution.py:22
  414.4 5.7 %collective-permute-start.70 = (f32[1,4,18,1]{3,2,1,0:T(8,128)S(1)}, f32[1,4,18,1]{3,2,1,0:T(8,128)S(1)}, u32[]{:S(2)}, u32[]{:S(2)}) collective-permute-start(f32[1,4,18,1]{3,2,1,0:T(8,128)S(1)} %get-tuple-element.91), channel_id=1, source_target_pairs={{1,0},{3,2},{5,4},{7,6},{9,8},{11,10},{13,12},{15,14},{17,16},{19,... | collective-permute-start | bytes 872 | tf_op jit(solution)/shard_map/ppermute | solution.py:24
  438.8 5.9 %collective-permute-start.76 = (f32[1,6,34,1]{3,0,2,1:T(1,128)S(1)}, f32[1,6,34,1]{3,0,2,1:T(1,128)S(1)}, u32[]{:S(2)}, u32[]{:S(2)}) collective-permute-start(f32[1,6,34,1]{3,0,2,1:T(1,128)S(1)} %get-tuple-element.65), channel_id=1, source_target_pairs={{1,0},{3,2},{5,4},{7,6},{9,8},{11,10},{13,12},{15,14},{17,16},{19,... | collective-permute-start | bytes 2456 | tf_op jit(solution)/shard_map/ppermute | solution.py:24
  463.2 6.0 %collective-permute-start.82 = (f32[1,6,34,1]{3,0,2,1:T(1,128)S(1)}, f32[1,6,34,1]{3,0,2,1:T(1,128)S(1)}, u32[]{:S(2)}, u32[]{:S(2)}) collective-permute-start(f32[1,6,34,1]{3,0,2,1:T(1,128)S(1)} %get-tuple-element.61), channel_id=1, source_target_pairs={{1,0},{3,2},{5,4},{7,6},{9,8},{11,10},{13,12},{15,14},{17,16},{19,... | collective-permute-start | bytes 2456 | tf_op jit(solution)/shard_map/ppermute | solution.py:24
  492.7 5.6 collective-permute-start.85
  504.5 6.0 %collective-permute-start.89 = (f32[1,10,66,1]{3,2,1,0:T(8,128)S(1)}, f32[1,10,66,1]{3,2,1,0:T(8,128)S(1)}, u32[]{:S(2)}, u32[]{:S(2)}) collective-permute-start(f32[1,10,66,1]{3,2,1,0:T(8,128)S(1)} %get-tuple-element.26), channel_id=1, source_target_pairs={{0,1},{2,3},{4,5},{6,7},{8,9},{10,11},{12,13},{14,15},{16,17},{18,... | collective-permute-start | bytes 7928 | tf_op jit(solution)/shard_map/ppermute | solution.py:22
  505.8 6.0 %collective-permute-start.88 = (f32[1,10,66,1]{3,2,1,0:T(8,128)S(1)}, f32[1,10,66,1]{3,2,1,0:T(8,128)S(1)}, u32[]{:S(2)}, u32[]{:S(2)}) collective-permute-start(f32[1,10,66,1]{3,2,1,0:T(8,128)S(1)} %get-tuple-element.25), channel_id=1, source_target_pairs={{1,0},{3,2},{5,4},{7,6},{9,8},{11,10},{13,12},{15,14},{17,16},{19,... | collective-permute-start | bytes 7928 | tf_op jit(solution)/shard_map/ppermute | solution.py:24
  514.2 5.6 collective-permute-start.91
  526.0 6.2 %collective-permute-start.95 = (f32[1,10,66,1]{3,2,1,0:T(8,128)S(1)}, f32[1,10,66,1]{3,2,1,0:T(8,128)S(1)}, u32[]{:S(2)}, u32[]{:S(2)}) collective-permute-start(f32[1,10,66,1]{3,2,1,0:T(8,128)S(1)} %get-tuple-element.24), channel_id=1, source_target_pairs={{0,1},{2,3},{4,5},{6,7},{8,9},{10,11},{12,13},{14,15},{16,17},{18,... | collective-permute-start | bytes 7928 | tf_op jit(solution)/shard_map/ppermute | solution.py:22
  527.3 6.2 %collective-permute-start.94 = (f32[1,10,66,1]{3,2,1,0:T(8,128)S(1)}, f32[1,10,66,1]{3,2,1,0:T(8,128)S(1)}, u32[]{:S(2)}, u32[]{:S(2)}) collective-permute-start(f32[1,10,66,1]{3,2,1,0:T(8,128)S(1)} %get-tuple-element.23), channel_id=1, source_target_pairs={{1,0},{3,2},{5,4},{7,6},{9,8},{11,10},{13,12},{15,14},{17,16},{19,... | collective-permute-start | bytes 7928 | tf_op jit(solution)/shard_map/ppermute | solution.py:24
  535.8 5.6 collective-permute-start.97
  547.6 6.2 %collective-permute-start.101 = (f32[1,10,66,1]{3,2,1,0:T(8,128)S(1)}, f32[1,10,66,1]{3,2,1,0:T(8,128)S(1)}, u32[]{:S(2)}, u32[]{:S(2)}) collective-permute-start(f32[1,10,66,1]{3,2,1,0:T(8,128)S(1)} %get-tuple-element.22), channel_id=1, source_target_pairs={{0,1},{2,3},{4,5},{6,7},{8,9},{10,11},{12,13},{14,15},{16,17},{18,... | collective-permute-start | bytes 7928 | tf_op jit(solution)/shard_map/ppermute | solution.py:22
  548.9 6.2 %collective-permute-start.100 = (f32[1,10,66,1]{3,2,1,0:T(8,128)S(1)}, f32[1,10,66,1]{3,2,1,0:T(8,128)S(1)}, u32[]{:S(2)}, u32[]{:S(2)}) collective-permute-start(f32[1,10,66,1]{3,2,1,0:T(8,128)S(1)} %get-tuple-element.21), channel_id=1, source_target_pairs={{1,0},{3,2},{5,4},{7,6},{9,8},{11,10},{13,12},{15,14},{17,16},{19,... | collective-permute-start | bytes 7928 | tf_op jit(solution)/shard_map/ppermute | solution.py:24
  (80 other events, 1337.3 us)
where the time goes:
time: 565 us; the launch traced here: 556 us
  starting transfers between devices  263 us (47%)
  local copies, waits for them, and re-layouts  134 us (24%)
  waiting for transfers between devices  82.3 us (15%)
  other arithmetic  74.7 us (13%)
    ppermute x51, starting transfers between devices, padded_2(): lax.ppermute(head, axis, [((i + 1) % count, i) for i in range(ends)])  162 us
    ppermute x51, starting transfers between devices, padded_2(): lax.ppermute(tail, axis, [(i, (i + 1) % count) for i in range(ends)])  100 us
    ppermute x51, waiting for transfers between devices, padded_2(): lax.ppermute(tail, axis, [(i, (i + 1) % count) for i in range(ends)])  71.2 us
    broadcast_in_dim x6, local copies, waits for them, and re-layouts, prolong(): wide = jnp.broadcast_to(wide, lead + (s[-3], 2, s[-2], 2, s[-1], 2))  24.2 us
    reduce_sum x9, other arithmetic, face_x(): return b.reshape(n0, n1 // 2, 2, n2 // 2, 2).sum(axis=(2, 4))  24.1 us
    reshape x2, local copies, waits for them, and re-layouts, blocks(): a.reshape(lead + (s[-3] // 2, 2, s[-2] // 2, 2, s[-1] // 2, 2))  22.4 us
    slice x10, local copies, waits for them, and re-layouts, face_x(): b = a[offset::2]  21.5 us
    reduce_sum x8, other arithmetic, blocks(): a.reshape(lead + (s[-3] // 2, 2, s[-2] // 2, 2, s[-1] // 2, 2))  20.5 us
  transfers between devices with their start and end apart: 102, of which 42 were waited for; matrix products, arithmetic and copies ran while one was open for 23% of the time, Pallas kernels for 0%

commit v1 on v0

v1 whole, which is shorter than its diff:
```python
import functools

import jax
import jax.numpy as jnp
from jax import lax
from jax.experimental import pallas as pl
from jax.experimental.pallas import tpu as pltpu
from jax.sharding import PartitionSpec as P


DAMPING = 2.0 / 3.0
LANES = 128
WIDE = 256
HALO = 7
FAR = 3
F32 = jnp.float32
VMEM_LIMIT = 24 * 1024 * 1024


class Plan:
    def __init__(self, sizes, shape):
        self.gx, self.gy, self.gz = sizes
        self.px, self.ny, self.nz = shape
        self.nx = self.px * self.gx
        self.by = self.ny // self.gx
        self.blocks = self.gx * self.gy
        self.rows = self.by + 2 * HALO
        self.paired = self.gz == 2
        order = [0, 1, 3, 2] if self.gx == 4 else list(range(self.gx))
        self.place = [order.index(i) for i in range(self.gx)]
        self.order = order

    def device(self, block):
        j, q = divmod(block, self.gx)
        i = self.order[q if j % 2 == 0 else self.gx - 1 - q]
        return i * self.gy + j

    def part(self, i, odd):
        q = self.place[i]
        return q + odd * (self.gx - 1 - 2 * q)

    def block_here(self):
        i, j = lax.axis_index("gx"), lax.axis_index("gy")
        q = sum(jnp.where(i == k, self.place[k], 0) for k in range(self.gx))
        odd = lax.rem(j, 2)
        return j * self.gx + q + odd * (self.gx - 1 - 2 * q)


def x_up(a, s=1):
    return pltpu.roll(a, a.shape[0] - s, 0)


def x_down(a, s=1):
    return pltpu.roll(a, s, 0)


def z_up(a, g):
    return pltpu.roll(a, a.shape[1] - g, 1)


def z_down(a, g):
    return pltpu.roll(a, g, 1)


def inverse(a):
    r = pl.reciprocal(a, approx=True)
    return r * (2.0 - a * r)


def each(first, last, step, body):
    count = last + 1 - first
    if count <= 2 * step:
        for i in range(first, last + 1):
            body(i)
        return

    def go(c, _):
        for k in range(step):
            body(first + c * step + k)
        return 0

    lax.fori_loop(0, count // step, go, 0)
    for i in range(first + count // step * step, last + 1):
        body(i)


class Wide:
    def __init__(self, ref):
        self.ref = ref

    def __getitem__(self, key):
        r, xs = key if isinstance(key, tuple) else (key, slice(None))
        return jnp.concatenate([self.ref[r, 0, xs, :], self.ref[r, 1, xs, :]], axis=1)

    def __setitem__(self, key, value):
        r, xs = key if isinstance(key, tuple) else (key, slice(None))
        self.ref[r, 0, xs, :] = value[:, :LANES]
        self.ref[r, 1, xs, :] = value[:, LANES:]


class Level:
    def __init__(self, s, g, kx, ky, kz, d, w, f, step=2):
        self.s, self.g, self.step = s, g, step
        self.kx, self.ky, self.kz, self.d, self.w, self.f = kx, ky, kz, d, w, f

    def beside(self, u, r):
        here = u[r]
        kx, kz = self.kx[r], self.kz[r]
        a = kx * x_up(here, self.s) + x_down(kx * here, self.s)
        b = kz * z_up(here, self.g) + z_down(kz * here, self.g)
        return a + b + (self.ky[r + 1] * u[r + 1] + self.ky[r] * u[r - 1])

    def weigh(self, first, last):
        def body(r):
            self.w[r] = DAMPING * inverse(self.d[r])

        each(first, last, self.step, body)

    def first(self, u, first, last):
        def body(r):
            u[r] = self.w[r] * self.f[r]

        each(first, last, self.step, body)

    def sweep(self, u, v, first, last):
        def body(r):
            v[r] = (1.0 / 3.0) * u[r] + self.w[r] * (self.f[r] + self.beside(u, r))

        each(first, last, self.step, body)

    def residual(self, u, r):
        return self.f[r] + self.beside(u, r) - self.d[r] * u[r]

    def residual_pairs(self, u, out, first, count):
        def body(j):
            out[j] = self.residual(u, first + 2 * j) + self.residual(u, first + 2 * j + 1)

        each(0, count - 1, max(1, self.step // 2), body)


def z_pairs(low, g):
    return lambda a: a + jnp.where(low, z_up(a, g), z_down(a, g))


def coarse_coefficients(level, r, x_count):
    even, odd = pl.ds(0, x_count, stride=2), pl.ds(1, x_count, stride=2)
    g = level.g
    low = (lax.broadcasted_iota(jnp.int32, (x_count, WIDE), 1) & g) == 0
    z_pair = z_pairs(low, g)

    def all_x(ref, row):
        return ref[row, even] + ref[row, odd]

    kx = level.kx[r, odd] + level.kx[r + 1, odd]
    inner = level.kx[r, even] + level.kx[r + 1, even] + all_x(level.ky, r + 1)
    kz = all_x(level.kz, r) + all_x(level.kz, r + 1)
    d = all_x(level.d, r) + all_x(level.d, r + 1)
    d = d - 2.0 * (inner + jnp.where(low, kz, 0.0))
    return z_pair(kx), coarse_sum(level.ky, r + 2, x_count, g), jnp.where(low, z_up(kz, g), kz), z_pair(d)


def coarse_sum(ref, r, x_count, g):
    even, odd = pl.ds(0, x_count, stride=2), pl.ds(1, x_count, stride=2)
    low = (lax.broadcasted_iota(jnp.int32, (x_count, WIDE), 1) & g) == 0
    return z_pairs(low, g)(ref[r, even] + ref[r, odd])


def correct(u, v, e, t, x_count, first, last, to):
    def body(j):
        part = e[j]
        t[j, pl.ds(0, x_count, stride=2)] = part
        t[j, pl.ds(1, x_count, stride=2)] = part
        wide = t[j]
        r = to + 2 * (j - first)
        v[r] = u[r] + wide
        v[r + 1] = u[r + 1] + wide

    each(first, last, 2, body)


def split_dot(a, b):
    high = a.astype(jnp.bfloat16)
    rest = a - high.astype(F32)
    mid = rest.astype(jnp.bfloat16)
    low = (rest - mid.astype(F32)).astype(jnp.bfloat16)
    dot = functools.partial(jnp.dot, preferred_element_type=F32)
    return dot(high, b) + dot(mid, b) + dot(low, b)


def prepare_kernel(plan, phase_in, density_in, rhs_in, out, phase, density, rhs, sems):
    pairs = ((phase_in, phase), (density_in, density), (rhs_in, rhs))
    copies = [pltpu.make_async_copy(a, b, sems.at[k]) for k, (a, b) in enumerate(pairs)]
    for copy in copies:
        copy.start()
    for copy in copies:
        copy.wait()
    odd = lax.rem(lax.axis_index("gy"), 2)
    by, px = plan.by, plan.px
    for i in range(plan.gx):
        start = pl.multiple_of(plan.part(i, odd) * by, by)
        rows = pl.ds(start, by)
        for p in range(px):
            half = jnp.where(phase[p, rows, :] == 1, 500.0, 0.5).astype(F32)
            at = i * by * 2 * px + p
            out[pl.ds(at, by, stride=2 * px), :] = half * density[p, rows, :]
            out[pl.ds(at + px, by, stride=2 * px), :] = rhs[0, p, rows, :]


def down_kernel(plan, c, lo, hi, zc, zh, *refs):
    near_count = 1 if plan.paired else 2
    pack, nears, refs = refs[0], refs[1 : 1 + near_count], refs[1 + near_count :]
    kx0, ky0, kz0, d0, w0, f0, ub, kx1, ky1, kz1, w1, f1, u1 = [Wide(r) for r in refs[:13]]
    h0, ua, r0, uc, r1, d1 = [Wide(r) for r in refs[13:19]]
    stage = refs[19]
    nx, by, rows, gx = plan.nx, plan.by, plan.rows, plan.gx
    shape = (nx, WIDE)
    base = plan.block_here() * by - HALO
    y_count, z_count = plan.by * plan.blocks, plan.nz * plan.gz

    x = lax.broadcasted_iota(jnp.int32, shape, 0)
    lane = lax.broadcasted_iota(jnp.int32, shape, 1)
    core = lax.axis_index("gz")
    if plan.paired:
        z = lax.rem(core * LANES + lane, WIDE)
    else:
        z = core * LANES + jnp.where(lane < LANES + LANES // 2, lane, lane - WIDE)
    x_top, x_bottom = x == nx - 1, x == 0
    z_top, z_bottom = z == z_count - 1, z == 0
    z_shut = (z < 0) | (z >= z_count - 1)
    z_out = (z < 0) | (z >= z_count)

    def take(a, b, shift, r, to):
        def field(t):
            left = jnp.concatenate([a[s, r, t] for s in range(gx)], axis=0)
            right = jnp.concatenate([b[shift + s, r, t] for s in range(gx)], axis=0)
            return jnp.concatenate([left, right], axis=1)

        y = base + to
        h = jnp.where((y >= 0) & (y < y_count), field(0), 0.5)
        h0[to] = h if plan.paired else jnp.where(z_out, 0.5, h)
        f0[to] = field(1)

    each(0, HALO - 1, 2, lambda r: take(lo, zh, 0, r, r))
    each(0, by - 1, 2, lambda r: take(c, zc, 0, r, r + HALO))
    each(0, HALO - 1, 2, lambda r: take(hi, zh, gx, r, r + HALO + by))

    def is_open(r):
        y = base + r
        return (y >= 0) & (y < y_count - 1)

    def face_above(r, h):
        return inverse(h + jnp.where(base + r == y_count - 1, h, h0[r + 1]))

    below = face_above(0, h0[0])
    ky0[1] = jnp.where(is_open(0), below, 0.0)

    def faces(r, below):
        h = h0[r]
        alone = 0.5 * inverse(h)
        xu = inverse(h + jnp.where(x_top, h, x_up(h)))
        xd = jnp.where(x_bottom, alone, x_down(xu))
        yu = face_above(r, h)
        yd = jnp.where(base + r == 0, alone, below)
        zu = inverse(h + jnp.where(z_top, h, z_up(h, 1)))
        zd = jnp.where(z_bottom, alone, z_down(zu, 1))
        d = xu + xd + yu + yd + zu + zd
        w = DAMPING * inverse(d)
        kx0[r] = jnp.where(x_top, 0.0, xu)
        ky0[r + 1] = jnp.where(is_open(r), yu, 0.0)
        kz0[r] = jnp.where(z_shut, 0.0, zu)
        d0[r], w0[r] = d, w
        ua[r] = w * f0[r]
        return yu

    def two_faces(k, below):
        return faces(2 * k + 2, faces(2 * k + 1, below))

    lax.fori_loop(0, (rows - 2) // 2, two_faces, below)

    fine = Level(1, 1, kx0, ky0, kz0, d0, w0, f0)
    fine.sweep(ua, ub, 2, rows - 3)
    fine.residual_pairs(ub, r0, 3, by // 2 + 4)

    own = by // 2
    half_x = nx // 2
    middle = Level(1, 2, kx1, ky1, kz1, d1, w1, f1)
    ky1[1] = coarse_sum(ky0, 1, half_x, 1)

    def coarsen(j):
        kx1[j], ky1[j + 1], kz1[j], d1[j] = coarse_coefficients(fine, 2 * j - 1, half_x)

    each(1, own + 6, 1, coarsen)

    def restrict(j):
        f1[j] = coarse_sum(r0, j - 2, half_x, 1)

    each(2, own + 5, 2, restrict)
    middle.weigh(1, own + 6)
    middle.first(uc, 2, own + 5)
    middle.sweep(uc, u1, 3, own + 4)
    middle.residual_pairs(u1, r1, 4, own // 2)

    quarter_x = nx // 4
    own2 = own // 2
    part = own2 // 2
    for j in range(own2):
        fields = (coarse_sum(r1, j, quarter_x, 2),) + coarse_coefficients(middle, 4 + 2 * j, quarter_x)
        for t, a in enumerate(fields):
            stage[j // part, pl.ds((t * part + j % part) * quarter_x, quarter_x), :] = a
    lane = lax.broadcasted_iota(jnp.int32, (WIDE, LANES), 0)
    cell = lax.broadcasted_iota(jnp.int32, (WIDE, LANES), 1)
    total = jnp.zeros(pack.shape, F32)
    for k in range(2):
        pick = jnp.where(lane == 4 * (cell - k * (WIDE // 4)), 1.0, 0.0).astype(jnp.bfloat16)
        total = total + split_dot(stage[k], pick)
    pack[...] = total

    size = pack.shape[0]

    def near(out, first):
        out[pl.ds(0, size), :] = total
        for k, (ref, r) in enumerate(((u1, first), (u1, first + 1), (u1, first + 2), (f1, first + 1))):
            for s in range(2):
                out[pl.ds(size + (2 * k + s) * half_x, half_x), :] = ref.ref[r, s]

    top = own
    if plan.paired:
        near(nears[0], top - (top - 5) * core)
    else:
        near(nears[0], top)
        near(nears[1], 5)


def up_kernel(plan, pack, below, above, *refs):
    refs, out, scratch = refs[:13], refs[13], refs[14:]
    kx0, ky0, kz0, d0, w0, f0, u0, kx1, ky1, kz1, w1, f1_in, u1_in = [Wide(r) for r in refs]
    stage = scratch[0]
    wide = [Wide(r) for r in scratch[1:]]
    f2, kx2, ky2, kz2, d2, w2, ua2, ub2, r2 = wide[:9]
    f3, kx3, ky3, kz3, d3, w3, ua3, ub3 = wide[9:17]
    t1, t0, f1, ua1, ub1, ua0, ub0 = wide[17:]
    nx, by = plan.nx, plan.by
    own, own2 = by // 2, by // 4
    part = own2 // 2
    half_x, quarter_x = nx // 2, nx // 4
    size = pack.shape[0]
    side = size + 8 * half_x
    core = lax.axis_index("gz")
    block = plan.block_here()
    zero = jnp.int32(0)

    for r in range(2, own + 6):
        f1[r] = f1_in[r]
    for r in range(3, own + 5):
        ua1[r] = u1_in[r]

    def spread_out(lower, upper, turn_lower, turn_upper):
        for k in range(FAR):
            at = 0 if k == 0 else side + (k - 1) * size
            stage[FAR - 1 - k] = lower[pl.ds(at, size), :]
            stage[FAR + 1 + k] = upper[pl.ds(at, size), :]
        for k, (ref, r_low, r_up) in enumerate(
            ((ua1, 0, own + 5), (ua1, 1, own + 6), (ua1, 2, own + 7), (f1, 1, own + 6))
        ):
            for s in range(2):
                rows = pl.ds(size + (2 * k + s) * half_x, half_x)
                ref.ref[r_low, s ^ turn_lower] = lower[rows, :]
                ref.ref[r_up, s ^ turn_upper] = upper[rows, :]

    stage[FAR] = pack[...]
    if plan.paired:
        turn_lower, turn_upper = core, 1 - core

        @pl.when(core == 0)
        def _():
            spread_out(below, above, 0, 1)

        @pl.when(core != 0)
        def _():
            spread_out(above, below, 1, 0)
    else:
        turn_lower, turn_upper = zero, zero
        spread_out(below, above, 0, 0)

    cell = lax.broadcasted_iota(jnp.int32, (LANES, 2 * WIDE), 0)
    lane = lax.broadcasted_iota(jnp.int32, (LANES, 2 * WIDE), 1)
    spread = jnp.where(cell == lax.div(lane, 4), 1.0, 0.0).astype(jnp.bfloat16)

    def expand(k):
        there = block + k - FAR
        exists = (there >= 0) & (there < plan.blocks)
        turn = jnp.where(k < FAR, turn_lower, jnp.where(k > FAR, turn_upper, 0))
        rows = split_dot(stage[k], spread)
        for t, ref in enumerate((f2, kx2, ky2, kz2, d2)):
            for j in range(own2):
                at = (t * part + j % part) * quarter_x
                a = rows[at : at + quarter_x, (j // part) * WIDE : (j // part + 1) * WIDE]
                if t == 4:
                    a = jnp.where(exists, a, 1.0)
                r = k * own2 + j + (1 if t == 2 else 0)
                ref.ref[r, turn] = a[:, :LANES]
                ref.ref[r, 1 - turn] = a[:, LANES:]

    each(0, 2 * FAR, 1, expand)

    rows2 = (2 * FAR + 1) * own2
    two = Level(1, 4, kx2, ky2, kz2, d2, w2, f2, 4)
    two.weigh(0, rows2 - 1)
    two.first(ua2, 0, rows2 - 1)
    two.sweep(ua2, ub2, 1, rows2 - 2)
    two.residual_pairs(ub2, r2, 2, rows2 // 2 - 2)

    x = lax.broadcasted_iota(jnp.int32, (quarter_x, WIDE), 0)
    even_x = (x & 1) == 0
    low = (lax.broadcasted_iota(jnp.int32, (quarter_x, WIDE), 1) & 4) == 0
    z_pair = z_pairs(low, 4)

    def x_pair(a):
        return a + jnp.where(even_x, x_up(a), x_down(a))

    last3 = rows2 // 2 - 2

    def coarsen(j):
        r = 2 * j
        kx = kx2[r] + kx2[r + 1]
        kz = kz2[r] + kz2[r + 1]
        inner = ky2[r + 1] + jnp.where(even_x, kx, 0.0) + jnp.where(low, kz, 0.0)
        f3[j] = z_pair(x_pair(r2[j - 1]))
        kx3[j] = z_pair(jnp.where(even_x, x_up(kx), kx))
        ky3[j + 1] = z_pair(x_pair(ky2[r + 2]))
        kz = x_pair(kz)
        kz3[j] = jnp.where(low, z_up(kz, 4), kz)
        d3[j] = z_pair(x_pair(d2[r] + d2[r + 1] - 2.0 * inner))

    each(1, last3, 2, coarsen)
    three = Level(2, 8, kx3, ky3, kz3, d3, w3, f3, 4)
    three.weigh(1, last3)
    three.first(ua3, 1, last3)
    three.sweep(ua3, ub3, 2, last3 - 1)
    three.sweep(ub3, ua3, 3, last3 - 2)
    three.sweep(ua3, ub3, 4, last3 - 3)

    first2 = FAR * own2
    for j in range(4, last3 - 2):
        e = ub3[j]
        ua2[2 * j] = ub2[2 * j] + e
        ua2[2 * j + 1] = ub2[2 * j + 1] + e
    two.sweep(ua2, ub2, first2 - 3, first2 + own2 + 2)
    two.sweep(ub2, ua2, first2 - 2, first2 + own2 + 1)

    one = Level(1, 2, kx1, ky1, kz1, None, w1, f1)
    correct(ua1, ub1, ua2, t1, quarter_x, first2 - 2, first2 + own2 + 1, 0)
    one.sweep(ub1, ua1, 1, own + 6)
    one.sweep(ua1, ub1, 2, own + 5)

    finest = Level(1, 1, kx0, ky0, kz0, d0, w0, f0)
    correct(u0, ua0, ub1, t0, half_x, 2, own + 5, 3)
    finest.sweep(ua0, ub0, HALO - 2, HALO + by + 1)
    finest.sweep(ub0, ua0, HALO - 1, HALO + by)

    def finish(r):
        scaled = d0[r] * ua0[r]
        rest = f0[r] + finest.beside(ua0, r) - scaled
        for s in range(plan.gx):
            part = slice(s * plan.px, (s + 1) * plan.px)
            out[s, r - HALO, 0] = scaled[part, :LANES]
            out[s, r - HALO, 1] = rest[part, :LANES]

    each(HALO, HALO + by - 1, 2, finish)


def place_kernel(plan, parts, scaled, residual):
    odd = lax.rem(lax.axis_index("gy"), 2)
    by, px = plan.by, plan.px
    for i in range(plan.gx):
        start = pl.multiple_of(plan.part(i, odd) * by, by)
        for p in range(px):
            at = i * by * 2 * px + p
            scaled[0, p, pl.ds(start, by), :] = parts[pl.ds(at, by, stride=2 * px), :]
            residual[0, p, pl.ds(start, by), :] = parts[pl.ds(at + px, by, stride=2 * px), :]


def in_vmem(*shape):
    return pltpu.VMEM(shape, F32)


def call(kernel, out_shape, scratch=(), **more):
    return pl.pallas_call(
        kernel,
        out_shape=out_shape,
        scratch_shapes=list(scratch),
        compiler_params=pltpu.CompilerParams(vmem_limit_bytes=VMEM_LIMIT),
        **more,
    )


def pinned(*arrays):
    return [pltpu.with_memory_space_constraint(a, pltpu.VMEM) for a in arrays]


def beside_in_z(plan, a):
    count = plan.gz
    if plan.paired:
        return lax.ppermute(a, "gz", [(0, 1), (1, 0)])
    cut = LANES // 2
    right = lax.ppermute(a[..., :cut], "gz", [(i + 1, i) for i in range(count - 1)])
    left = lax.ppermute(a[..., cut:], "gz", [(i, i + 1) for i in range(count - 1)])
    return jnp.concatenate([right, left], axis=-1)


def shift(plan, a, k):
    pairs = [(plan.device(b), plan.device(b + k)) for b in range(plan.blocks) if 0 <= b + k < plan.blocks]
    return lax.ppermute(a, ("gx", "gy"), pairs)


def shift_apart(plan, a, k):
    pairs = []
    for b in range(plan.blocks):
        for core, to in ((0, b + k), (1, b - k)):
            if 0 <= to < plan.blocks:
                pairs.append((2 * plan.device(b) + core, 2 * plan.device(to) + core))
    return lax.ppermute(a, ("gx", "gy", "gz"), pairs)


def on_device(plan, phase, density, rhs):
    nx, by, rows, px, gx = plan.nx, plan.by, plan.rows, plan.px, plan.gx
    flat = gx * by * 2 * px
    block = (px, plan.ny, LANES)
    anywhere = pl.BlockSpec(memory_space=pl.ANY)
    (parts,) = call(
        functools.partial(prepare_kernel, plan),
        [in_vmem(flat, LANES)],
        [pltpu.VMEM(block, jnp.int32), in_vmem(*block), in_vmem(1, *block), pltpu.SemaphoreType.DMA((3,))],
        in_specs=[anywhere] * 3,
    )(phase, density, rhs)
    parts = parts.reshape(gx, by, 2, px, LANES)
    c = lax.all_to_all(parts, "gx", 0, 0, tiled=True)
    lo = shift(plan, c[:, by - HALO :], 1)
    hi = shift(plan, c[:, :HALO], -1)
    zc = beside_in_z(plan, c)
    zh = beside_in_z(plan, jnp.concatenate([lo, hi], axis=0))

    own, own2 = by // 2, by // 4
    size = 5 * (own2 // 2) * (nx // 4)
    side = size + 8 * (nx // 2)

    def level0(n):
        return in_vmem(n, 2, nx, LANES)

    def level1(n):
        return in_vmem(n, 2, nx // 2, LANES)

    outs = [in_vmem(size, LANES)] + [in_vmem(side, LANES)] * (1 if plan.paired else 2)
    fields = [level0(rows)] * 7 + [level1(own + 8)] * 6
    scratch = [level0(rows)] * 2 + [level0(own + 4), level1(own + 8), level1(own2), level1(own + 8)]
    scratch += [in_vmem(2, size, WIDE)]
    down = call(functools.partial(down_kernel, plan), outs + fields, scratch)(*pinned(c, lo, hi, zc, zh))
    pack, nears, fields = down[0], down[1 : len(outs)], down[len(outs) :]

    if plan.paired:
        mine = [shift_apart(plan, a, k + 1) for k, a in enumerate([nears[0]] + [pack] * (FAR - 1))]
        below = jnp.concatenate(mine, axis=0)
        above = lax.ppermute(below, "gz", [(0, 1), (1, 0)])
    else:
        below = jnp.concatenate(
            [shift(plan, a, k + 1) for k, a in enumerate([nears[0]] + [pack] * (FAR - 1))], axis=0
        )
        above = jnp.concatenate(
            [shift(plan, a, -k - 1) for k, a in enumerate([nears[1]] + [pack] * (FAR - 1))], axis=0
        )

    rows2 = (2 * FAR + 1) * own2
    scratch = [in_vmem(2 * FAR + 1, size, LANES)]
    scratch += [in_vmem(rows2 + 1, 2, nx // 4, LANES)] * 9 + [in_vmem(rows2 // 2 + 1, 2, nx // 4, LANES)] * 8
    scratch += [level1(rows2), level0(own + 8)] + [level1(own + 8)] * 3 + [level0(rows)] * 2
    (result,) = call(
        functools.partial(up_kernel, plan), [in_vmem(gx, by, 2, px, LANES)], scratch
    )(*pinned(pack, below, above, *fields))

    result = lax.all_to_all(result, "gx", 0, 0, tiled=True)
    return call(
        functools.partial(place_kernel, plan),
        [jax.ShapeDtypeStruct((1, px, plan.ny, LANES), F32)] * 2,
    )(*pinned(result.reshape(flat, LANES)))


def solution(mesh):
    sizes = [mesh.shape[a] for a in ("gx", "gy", "gz")]

    def local(phase, density, rhs):
        return tuple(on_device(Plan(sizes, phase.shape), phase, density, rhs))

    in_specs = (P("gx", "gy", "gz"), P("gx", "gy", "gz"), P(None, "gx", "gy", "gz"))
    out_specs = (P(None, "gx", "gy", "gz"), P(None, "gx", "gy", "gz"))
    return jax.shard_map(local, mesh=mesh, in_specs=in_specs, out_specs=out_specs, check_vma=False)
```

time: 565 us -> 75.5 us (0.13)
  the two profiles are of different devices: /device:TPU:29 before, /device:TPU:0 now
where the time goes in v1:
time: 75.5 us; the launch traced here: 75.2 us
  blocking collectives  27.5 us (36%)
  Pallas kernels  18.9 us (25%)
  starting transfers between devices  16.8 us (22%)
  waiting for transfers between devices  8.27 us (11%)
  local copies, waits for them, and re-layouts  2.89 us (4%)
  between operations  0.77 us (1%)
    all_to_all x1, blocking collectives, on_device(): result = lax.all_to_all(result, 'gx', 0, 0, tiled=True)  14 us
    all_to_all x1, blocking collectives, on_device(): c = lax.all_to_all(parts, 'gx', 0, 0, tiled=True)  13.5 us
    ppermute x3, starting transfers between devices, shift_apart(): return lax.ppermute(a, ('gx', 'gy', 'gz'), pairs)  10.7 us
    pallas_call x1, Pallas kernels, on_device(): call(functools.partial(down_kernel, plan), outs + fields, scratch)  8.98 us
    pallas_call x1, Pallas kernels, on_device(): call(functools.partial(up_kernel, plan), [in_vmem(gx, by, 2, px, LANES)],...  8.71 us
    ppermute x2, starting transfers between devices, shift(): return lax.ppermute(a, ('gx', 'gy'), pairs)  5.85 us
    ppermute x2, waiting for transfers between devices, shift(): return lax.ppermute(a, ('gx', 'gy'), pairs)  3.43 us
    unnamed x8, local copies, waits for them, and re-layouts  2.86 us
  transfers between devices with their start and end apart: 8, of which 5 were waited for; matrix products, arithmetic and copies ran while one was open for 0% of the time, Pallas kernels for 0%

profile of v1, /device:TPU:0, one launch (start us, length us, event | category | flops | bytes accessed | tf_op | source)
XLA Modules:
  0.0 75.2 jit_solution(8378182867204175030)
XLA Ops:
  0.6 0.0 copy-start
  0.6 0.9 %copy-done = s32[8,64,128]{2,1,0:T(8,128)S(1)} copy-done((s32[8,64,128]{2,1,0:T(8,128)S(1)}, s32[8,64,128]{2,1,0:T(8,128)}, u32[]{:S(2)}) %copy-start) | copy-done | bytes 262168
  1.6 0.0 copy-start.1
  1.6 0.9 %copy-done.1 = f32[8,64,128]{2,1,0:T(8,128)S(1)} copy-done((f32[8,64,128]{2,1,0:T(8,128)S(1)}, f32[8,64,128]{2,1,0:T(8,128)}, u32[]{:S(2)}) %copy-start.1) | copy-done | bytes 262168
  2.5 0.0 copy-start.2
  2.5 0.9 %copy-done.2 = f32[1,8,64,128]{3,2,1,0:T(8,128)S(1)} copy-done((f32[1,8,64,128]{3,2,1,0:T(8,128)S(1)}, f32[1,8,64,128]{3,2,1,0:T(8,128)}, u32[]{:S(2)}) %copy-start.2) | copy-done | bytes 262168
  3.5 0.3 shard_map.50
  3.8 13.5 %all_to_all.10.c = f32[4,16,2,8,128]{4,3,2,1,0:T(8,128)S(1)} all-to-all(f32[4,16,2,8,128]{4,3,2,1,0:T(8,128)S(1)} %bitcast.3), channel_id=1, replica_groups=mesh['gx'=4,'gy'=4,'gz'=2] {'gx'}, dimensions={0} | all-to-all | bytes 1048576 | tf_op jit(solution)/shard_map/all_to_all | solution.py:537
  17.3 1.3 %collective-permute-start.1 = (f32[4,7,2,8,128]{4,3,2,1,0:T(8,128)S(1)}, f32[4,7,2,8,128]{4,3,2,1,0:T(8,128)S(1)}, u32[]{:S(2)}, u32[]{:S(2)}) collective-permute-start(f32[4,7,2,8,128]{4,3,2,1,0:T(8,128)S(1)} %get-tuple-element.32), channel_id=1, source_target_pairs={{8,0},{24,8},{16,24},{18,16},{26,18},{10,26},{2,10},{4,2},{12,4},{... | collective-permute-start | bytes 688136 | tf_op jit(solution)/shard_map/ppermute | solution.py:513
  18.6 4.6 %collective-permute-start = (f32[4,7,2,8,128]{4,3,2,1,0:T(8,128)S(1)}, f32[4,7,2,8,128]{4,3,2,1,0:T(8,128)S(1)}, u32[]{:S(2)}, u32[]{:S(2)}) collective-permute-start(f32[4,7,2,8,128]{4,3,2,1,0:T(8,128)S(1)} %get-tuple-element.33), channel_id=1, source_target_pairs={{0,8},{8,24},{24,16},{16,18},{18,26},{26,10},{10,2},{2,4},{4,12},{... | collective-permute-start | bytes 688136 | tf_op jit(solution)/shard_map/ppermute | solution.py:513
  23.2 0.1 collective-permute-start.2
  23.2 2.0 %collective-permute-done.1.hi = f32[4,7,2,8,128]{4,3,2,1,0:T(8,128)S(1)} collective-permute-done((f32[4,7,2,8,128]{4,3,2,1,0:T(8,128)S(1)}, f32[4,7,2,8,128]{4,3,2,1,0:T(8,128)S(1)}, u32[]{:S(2)}, u32[]{:S(2)}) %collective-permute-start.1) | collective-permute-done | bytes 229408 | tf_op jit(solution)/shard_map/ppermute | solution.py:513
  25.2 1.5 %collective-permute-done.lo = f32[4,7,2,8,128]{4,3,2,1,0:T(8,128)S(1)} collective-permute-done((f32[4,7,2,8,128]{4,3,2,1,0:T(8,128)S(1)}, f32[4,7,2,8,128]{4,3,2,1,0:T(8,128)S(1)}, u32[]{:S(2)}, u32[]{:S(2)}) %collective-permute-start) | collective-permute-done | bytes 229408 | tf_op jit(solution)/shard_map/ppermute | solution.py:513
  26.7 0.1 collective-permute-start.3
  26.8 0.0 collective-permute-done.2.zc
  26.8 1.8 %collective-permute-done.3.zh = f32[8,7,2,8,128]{4,3,2,1,0:T(8,128)S(1)} collective-permute-done((f32[8,7,2,8,128]{4,3,2,1,0:T(8,128)S(1)}, f32[8,7,2,8,128]{4,3,2,1,0:T(8,128)S(1)}, u32[]{:S(2)}, u32[]{:S(2)}) %collective-permute-start.3) | collective-permute-done | bytes 458784 | tf_op jit(solution)/shard_map/ppermute | solution.py:504
  28.6 9.0 %shard_map.51 = (f32[80,128]{1,0:T(8,128)S(1)}, f32[208,128]{1,0:T(8,128)S(1)}, f32[30,2,32,128]{3,2,1,0:T(8,128)S(1)}, f32[30,2,32,128]{3,2,1,0:T(8,128)S(1)}, ...) custom-call(f32[4,16,2,8,128]{4,3,2,1,0:T(8,128)S(1)} %all_to_all.10, ...), custom_call_target="tpu_custom_call" | custom-call | tf_op jit(solution)/shard_map/pallas_call | solution.py:557
  37.6 4.4 %collective-permute-start.4 = (f32[208,128]{1,0:T(8,128)S(1)}, f32[208,128]{1,0:T(8,128)S(1)}, u32[]{:S(2)}, u32[]{:S(2)}) collective-permute-start(f32[208,128]{1,0:T(8,128)S(1)} %get-tuple-element.18), channel_id=1, source_target_pairs={{0,8},{8,24},{9,1},{24,16},{25,9},{16,18},{17,25},{18,26},{19,17},... | collective-permute-start | bytes 319496 | tf_op jit(solution)/shard_map/ppermute | solution.py:522
  42.0 2.8 %collective-permute-start.6 = (f32[80,128]{1,0:T(8,128)S(1)}, f32[80,128]{1,0:T(8,128)S(1)}, u32[]{:S(2)}, u32[]{:S(2)}) collective-permute-start(f32[80,128]{1,0:T(8,128)S(1)} %get-tuple-element.17.pack), channel_id=1, source_target_pairs={{0,16},{8,18},{24,26},{16,10},{17,1},{18,2},{19,9},{26,4},{27,25},... | collective-permute-start | bytes 122888 | tf_op jit(solution)/shard_map/ppermute | solution.py:522
  44.8 3.5 %collective-permute-start.5 = (f32[80,128]{1,0:T(8,128)S(1)}, f32[80,128]{1,0:T(8,128)S(1)}, u32[]{:S(2)}, u32[]{:S(2)}) collective-permute-start(f32[80,128]{1,0:T(8,128)S(1)} %get-tuple-element.17.pack), channel_id=1, source_target_pairs={{0,24},{8,16},{24,18},{25,1},{16,26},{17,9},{18,10},{19,25},{26,2}... | collective-permute-start | bytes 122888 | tf_op jit(solution)/shard_map/ppermute | solution.py:522
  48.3 0.0 collective-permute-done.4
  48.3 1.6 %collective-permute-done.5 = f32[80,128]{1,0:T(8,128)S(1)} collective-permute-done((f32[80,128]{1,0:T(8,128)S(1)}, f32[80,128]{1,0:T(8,128)S(1)}, u32[]{:S(2)}, u32[]{:S(2)}) %collective-permute-start.5) | collective-permute-done | bytes 40992 | tf_op jit(solution)/shard_map/ppermute | solution.py:522
  50.0 0.0 collective-permute-done.6
  50.0 0.1 collective-permute-start.7
  50.0 1.4 %collective-permute-done.7.above = f32[368,128]{1,0:T(8,128)S(1)} collective-permute-done((f32[368,128]{1,0:T(8,128)S(1)}, f32[368,128]{1,0:T(8,128)S(1)}, u32[]{:S(2)}, u32[]{:S(2)}) %collective-permute-start.7) | collective-permute-done | bytes 188448 | tf_op jit(solution)/shard_map/ppermute | solution.py:563
  51.5 8.7 %shard_map.52 = f32[4,16,2,8,128]{4,3,2,1,0:T(8,128)S(1)} custom-call(f32[80,128]{1,0:T(8,128)S(1)} %get-tuple-element.17.pack, f32[368,128]{1,0:T(8,128)S(1)} %constant_dynamic-update-slice_fusion.below, f32[368,128]{1,0:T(8,128)S(1)} %collective-permute-done.7.above, f32[30,2,32,128]{3,2,1,0:T(8,128)S(1)} %get-tuple-element.19.refs_0_, ...), custom_call_target="tpu_custom_call" | custom-call | tf_op jit(solution)/shard_map/pallas_call | solution.py:576
  60.2 14.0 %all_to_all.11 = f32[4,16,2,8,128]{4,3,2,1,0:T(8,128)S(1)} all-to-all(f32[4,16,2,8,128]{4,3,2,1,0:T(8,128)S(1)} %shard_map.52), channel_id=1, replica_groups=mesh['gx'=4,'gy'=4,'gz'=2] {'gx'}, dimensions={0} | all-to-all | bytes 1048576 | tf_op jit(solution)/shard_map/all_to_all | solution.py:580
  74.2 0.9 %shard_map.53 = (f32[1,8,64,128]{3,2,1,0:T(8,128)}, f32[1,8,64,128]{3,2,1,0:T(8,128)}) custom-call(f32[1024,128]{1,0:T(8,128)S(1)} %bitcast.2), custom_call_target="tpu_custom_call" | custom-call | tf_op jit(solution)/shard_map/pallas_call | solution.py:581
  (5 shorter events, 0.1 us)
Async XLA Ops:
  0.6 1.0 %copy-start = (s32[8,64,128]{2,1,0:T(8,128)S(1)}, s32[8,64,128]{2,1,0:T(8,128)}, u32[]{:S(2)}) copy-start(s32[8,64,128]{2,1,0:T(8,128)} %phase_in.1) | copy-start | bytes 786436
  1.6 0.9 %copy-start.1 = (f32[8,64,128]{2,1,0:T(8,128)S(1)}, f32[8,64,128]{2,1,0:T(8,128)}, u32[]{:S(2)}) copy-start(f32[8,64,128]{2,1,0:T(8,128)} %density_in.1) | copy-start | bytes 786436
  2.5 0.9 %copy-start.2 = (f32[1,8,64,128]{3,2,1,0:T(8,128)S(1)}, f32[1,8,64,128]{3,2,1,0:T(8,128)}, u32[]{:S(2)}) copy-start(f32[1,8,64,128]{3,2,1,0:T(8,128)} %rhs_in.1) | copy-start | bytes 786436
  17.3 7.9 %collective-permute-start.1 = (f32[4,7,2,8,128]{4,3,2,1,0:T(8,128)S(1)}, f32[4,7,2,8,128]{4,3,2,1,0:T(8,128)S(1)}, u32[]{:S(2)}, u32[]{:S(2)}) collective-permute-start(f32[4,7,2,8,128]{4,3,2,1,0:T(8,128)S(1)} %get-tuple-element.32), channel_id=1, source_target_pairs={{8,0},{24,8},{16,24},{18,16},{26,18},{10,26},{2,10},{4,2},{12,4},{... | collective-permute-start | bytes 688136 | tf_op jit(solution)/shard_map/ppermute | solution.py:513
  18.6 8.1 %collective-permute-start = (f32[4,7,2,8,128]{4,3,2,1,0:T(8,128)S(1)}, f32[4,7,2,8,128]{4,3,2,1,0:T(8,128)S(1)}, u32[]{:S(2)}, u32[]{:S(2)}) collective-permute-start(f32[4,7,2,8,128]{4,3,2,1,0:T(8,128)S(1)} %get-tuple-element.33), channel_id=1, source_target_pairs={{0,8},{8,24},{24,16},{16,18},{18,26},{26,10},{10,2},{2,4},{4,12},{... | collective-permute-start | bytes 688136 | tf_op jit(solution)/shard_map/ppermute | solution.py:513
  23.2 3.6 %collective-permute-start.2 = (f32[4,16,2,8,128]{4,3,2,1,0:T(8,128)S(1)}, f32[4,16,2,8,128]{4,3,2,1,0:T(8,128)S(1)}, u32[]{:S(2)}, u32[]{:S(2)}) collective-permute-start(f32[4,16,2,8,128]{4,3,2,1,0:T(8,128)S(1)} %all_to_all.10.c), channel_id=1, source_target_pairs={{0,1},{1,0},{2,3},{3,2},{4,5},{5,4},{6,7},{7,6},{8,9},{9,8},{10,11... | collective-permute-start | bytes 1572872 | tf_op jit(solution)/shard_map/ppermute | solution.py:504
  26.7 1.9 %collective-permute-start.3 = (f32[8,7,2,8,128]{4,3,2,1,0:T(8,128)S(1)}, f32[8,7,2,8,128]{4,3,2,1,0:T(8,128)S(1)}, u32[]{:S(2)}, u32[]{:S(2)}) collective-permute-start(f32[8,7,2,8,128]{4,3,2,1,0:T(8,128)S(1)} %pad_maximum_fusion), channel_id=1, source_target_pairs={{0,1},{1,0},{2,3},{3,2},{4,5},{5,4},{6,7},{7,6},{8,9},{9,8},{10,11... | collective-permute-start | bytes 1376264 | tf_op jit(solution)/shard_map/ppermute | solution.py:504
  37.6 10.7 %collective-permute-start.4 = (f32[208,128]{1,0:T(8,128)S(1)}, f32[208,128]{1,0:T(8,128)S(1)}, u32[]{:S(2)}, u32[]{:S(2)}) collective-permute-start(f32[208,128]{1,0:T(8,128)S(1)} %get-tuple-element.18), channel_id=1, source_target_pairs={{0,8},{8,24},{9,1},{24,16},{25,9},{16,18},{17,25},{18,26},{19,17},... | collective-permute-start | bytes 319496 | tf_op jit(solution)/shard_map/ppermute | solution.py:522
  42.0 8.0 %collective-permute-start.6 = (f32[80,128]{1,0:T(8,128)S(1)}, f32[80,128]{1,0:T(8,128)S(1)}, u32[]{:S(2)}, u32[]{:S(2)}) collective-permute-start(f32[80,128]{1,0:T(8,128)S(1)} %get-tuple-element.17.pack), channel_id=1, source_target_pairs={{0,16},{8,18},{24,26},{16,10},{17,1},{18,2},{19,9},{26,4},{27,25},... | collective-permute-start | bytes 122888 | tf_op jit(solution)/shard_map/ppermute | solution.py:522
  44.8 5.1 %collective-permute-start.5 = (f32[80,128]{1,0:T(8,128)S(1)}, f32[80,128]{1,0:T(8,128)S(1)}, u32[]{:S(2)}, u32[]{:S(2)}) collective-permute-start(f32[80,128]{1,0:T(8,128)S(1)} %get-tuple-element.17.pack), channel_id=1, source_target_pairs={{0,24},{8,16},{24,18},{25,1},{16,26},{17,9},{18,10},{19,25},{26,2}... | collective-permute-start | bytes 122888 | tf_op jit(solution)/shard_map/ppermute | solution.py:522
  50.0 1.5 %collective-permute-start.7 = (f32[368,128]{1,0:T(8,128)S(1)}, f32[368,128]{1,0:T(8,128)S(1)}, u32[]{:S(2)}, u32[]{:S(2)}) collective-permute-start(f32[368,128]{1,0:T(8,128)S(1)} %constant_dynamic-update-slice_fusion.below), channel_id=1, source_target_pairs={{0,1},{1,0},{2,3},{3,2},{4,5},{5,4},{6,7},{7,6},{8,9},{9,8},{10,11... | collective-permute-start | bytes 565256 | tf_op jit(solution)/shard_map/ppermute | solution.py:563
